TPU v7x, 256 devices: a whole 4x4x8 slice. The times are simulated.
256 devices in a mesh: row: 16 (over x_hi, z), col: 8 (over x_lo, y), cores: 2 (over core).
Axes of the slice: x: 4 (x_hi: 2, x_lo: 2; x = x_hi * 2 + x_lo), y: 4, z: 8, core: 2. Of those that a mesh axis runs over, the one named last changes fastest.
Arguments:
- batch_index: int32 [32768], P(('row', 'col')), may hold values from 0 to 511, as said below
- chip_features: bfloat16 [65536, 2048], P(('row', 'col')), may hold values from -6 to 6
- head_weight: bfloat16 [2048, 128], replicated, may hold values from -0.125 to 0.125
- probe_left: bfloat16 [32768, 64], P(('row', 'col'), 'cores'), may hold values from -2.5 to 2.5
- probe_right: bfloat16 [32768, 64], P(('row', 'col'), 'cores'), may hold values from -2.5 to 2.5
Outputs:
- embed_grad: float32 [32768, 128], P(('row', 'col'))
- head_grad: float32 [2048, 128], replicated
Inputs may be any that keep to these rules, and one draw needn't show every extreme that they name: `batch_index`: within each aligned block of 256 points the indices are distinct; they count the chips held with that block, from its first one.
All inputs are finite; a program needn't handle non-finite values.
Results may differ from a plain program's by a relative error of at most 0.0041.
Values may be sent and summed in bfloat16 or wider, within the bound.
A program may use at most 64 MiB of HBM per device.

v0:
```python
import math

import jax
import jax.numpy as jnp
from jax import lax
from jax.sharding import PartitionSpec as P


def kernel_block(row_embed, row_square, col_embed):
    col_float = col_embed.astype(jnp.float32)
    col_square = jnp.sum(col_float * col_float, axis=1)
    products = lax.dot_general(
        row_embed, col_embed, (((1,), (1,)), ((), ())), preferred_element_type=jnp.float32
    )
    scale_factor = 0.5 / row_embed.shape[1]
    return jnp.exp(-(row_square[:, None] + col_square[None, :] - 2.0 * products) * scale_factor)


def probe_intersection(left_rows, right_rows):
    return lax.dot_general(
        left_rows, right_rows, (((1,), (1,)), ((), ())), preferred_element_type=jnp.float32
    )


def split_blocks(array_in, block_cols):
    return array_in.reshape(array_in.shape[0] // block_cols, block_cols, array_in.shape[1])


def local(batch_index, chip_features, head_weight, probe_left, probe_right):
    own_points = batch_index.shape[0]
    features = jnp.take(chip_features, batch_index, axis=0)
    embedding = jnp.dot(features, head_weight, preferred_element_type=jnp.float32).astype(
        jnp.bfloat16
    )
    embed_width = embedding.shape[1]
    inverse_width = 1.0 / embed_width
    row_embed, row_left = (
        lax.all_gather(embedding, "col", axis=0, tiled=True),
        lax.all_gather(probe_left, "col", axis=0, tiled=True),
    )
    col_embed, col_right = (
        lax.all_gather(embedding, "row", axis=0, tiled=True),
        lax.all_gather(probe_right, "row", axis=0, tiled=True),
    )
    row_float = row_embed.astype(jnp.float32)
    row_square = jnp.sum(row_float * row_float, axis=1)
    col_count = col_embed.shape[0]
    block_cols = min(512, col_count)

    def tile_scattered(totals, inputs):
        row_total, row_mass = totals
        block_embed, block_right = inputs
        weight_tile = (
            kernel_block(row_embed, row_square, block_embed)
            * probe_intersection(row_left, block_right)
            * inverse_width
        )
        rounded_tile = weight_tile.astype(jnp.bfloat16)
        row_total = row_total + jnp.dot(
            rounded_tile, block_embed, preferred_element_type=jnp.float32
        )
        row_mass = row_mass + jnp.sum(weight_tile, axis=1)
        col_part = lax.dot_general(
            rounded_tile, row_embed, (((0,), (0,)), ((), ())), preferred_element_type=jnp.float32
        ) - jnp.sum(weight_tile, axis=0)[:, None] * block_embed.astype(jnp.float32)
        return ((row_total, row_mass), col_part)

    start_totals = (
        jnp.zeros(row_float.shape, jnp.float32),
        jnp.zeros((row_float.shape[0],), jnp.float32),
    )
    (row_total, row_mass), col_parts = lax.scan(
        tile_scattered,
        start_totals,
        (split_blocks(col_embed, block_cols), split_blocks(col_right, block_cols)),
    )
    row_part = row_total - row_mass[:, None] * row_float
    col_part = col_parts.reshape(col_count, embed_width)
    owned = lax.psum_scatter(row_part, "col", scatter_dimension=0, tiled=True) + lax.psum_scatter(
        col_part, "row", scatter_dimension=0, tiled=True
    )
    embed_grad = lax.psum(owned, "cores")
    total_points = own_points * lax.axis_size("row") * lax.axis_size("col")
    norm_factor = 1.0 / math.sqrt(total_points)
    local_head = jnp.dot(
        features.astype(jnp.float32).T, embed_grad, precision=lax.Precision.HIGHEST
    )
    head_grad = lax.psum(local_head, ("row", "col")) * norm_factor
    return (embed_grad, head_grad)


def solution(mesh):
    return jax.shard_map(
        local,
        mesh=mesh,
        in_specs=(
            P(("row", "col")),
            P(("row", "col"), None),
            P(),
            P(("row", "col"), "cores"),
            P(("row", "col"), "cores"),
        ),
        out_specs=(P(("row", "col"), None), P()),
        check_vma=False,
    )
```

profile of v0, /device:TPU:1, one launch (start us, length us, event | category | flops | bytes accessed | tf_op | source)
XLA Modules:
  0.0 730.5 jit_solution(4525468828489415884)
XLA Ops:
  7.2 0.8 compare_select_fusion
  8.8 1.4 gather_fusion
  10.2 2.5 convolution_convert_fusion
  12.8 39.4 %all_gather.14 = bf16[4096,32]{0,1:T(8,128)(2,1)S(1)} all-gather(bf16[256,32]{0,1:T(8,128)(2,1)S(1)} %copy-done.5), channel_id=1, replica_groups=mesh['row'=16,'col'=8,'cores'=2] {'row'}, dimensions={0}, use_global_device_ids=true | all-gather | bytes 278528 | tf_op jit(solution)/shard_map/all_gather | solution.py:43
  52.2 1.3 copy.7
  53.6 26.3 %all_gather.15 = bf16[2048,32]{1,0:T(8,128)(2,1)} all-gather(bf16[256,32]{1,0:T(8,128)(2,1)S(1)} %copy.8), channel_id=1, replica_groups=mesh['row'=16,'col'=8,'cores'=2] {'col'}, dimensions={0}, use_global_device_ids=true | all-gather | bytes 147456 | tf_op jit(solution)/shard_map/all_gather | solution.py:39
  79.9 24.0 %all_gather.12 = bf16[2048,128]{1,0:T(8,128)(2,1)S(1)} all-gather(bf16[256,128]{1,0:T(8,128)(2,1)} %convolution_convert_fusion), channel_id=1, replica_groups=mesh['row'=16,'col'=8,'cores'=2] {'col'}, dimensions={0}, use_global_device_ids=true | all-gather | bytes 589824 | tf_op jit(solution)/shard_map/all_gather | solution.py:38
  104.4 101.1 %while.15 = (s32[]{:T(128)}, f32[2048,128]{1,0:T(8,128)}, f32[2048]{0:T(1024)S(1)}, f32[8,512,128]{2,1,0:T(8,128)}, f32[2048]{0:T(1024)S(1)}, /*index=5*/bf16[8,...) while((s32[]{:T(128)}, f32[2048,128]{1,0:T(8,128)}, ...), condition=%wide.region_5.6_spmd.clone, body=%wide.region_1.5_spmd.clone.sunk | while | flops 883819520 | bytes 27838640 | solution.py:72
  104.4 1.7 fusion.50
  106.1 1.1 fusion.51
  107.1 2.7 fusion.52
  109.8 1.3 copy-done.1
  111.1 2.3 fusion.53
  113.4 3.3 convolution_add_fusion.2
  116.7 1.7 fusion.50
  118.4 1.1 fusion.51
  119.5 2.7 fusion.52
  122.2 1.3 copy-done.1
  123.5 2.3 fusion.53
  125.8 3.6 convolution_add_fusion.2
  129.4 1.7 fusion.50
  131.1 1.1 fusion.51
  132.2 2.7 fusion.52
  134.8 1.3 copy-done.1
  136.1 2.3 fusion.53
  138.5 3.6 convolution_add_fusion.2
  142.1 1.7 fusion.50
  143.7 1.1 fusion.51
  144.8 2.7 fusion.52
  147.5 1.3 copy-done.1
  148.8 2.3 fusion.53
  151.1 3.6 convolution_add_fusion.2
  154.8 1.7 fusion.50
  156.4 1.1 fusion.51
  157.5 2.7 fusion.52
  160.2 1.3 copy-done.1
  161.5 2.3 fusion.53
  163.8 3.6 convolution_add_fusion.2
  167.4 1.7 fusion.50
  169.1 1.1 fusion.51
  170.2 2.7 fusion.52
  172.9 1.3 copy-done.1
  174.2 2.4 fusion.53
  176.5 3.6 convolution_add_fusion.2
  180.1 1.7 fusion.50
  181.8 1.1 fusion.51
  182.9 2.7 fusion.52
  185.6 1.3 copy-done.1
  186.9 2.3 fusion.53
  189.2 3.6 convolution_add_fusion.2
  192.8 1.7 fusion.50
  194.5 1.1 fusion.51
  195.6 2.7 fusion.52
  198.2 1.3 copy-done.1
  199.5 2.3 fusion.53
  201.9 3.6 convolution_add_fusion.2
  205.5 2.5 fusion.20
  208.8 47.5 %reduce-scatter.3.cloned.1.call-done = f32[256,128]{1,0:T(8,128)} async-done(((f32[2048,128]{1,0:T(8,128)}), f32[256,128]{1,0:T(8,128)}) %reduce-scatter.3.cloned.1.call-update) | async-done | bytes 131088 | tf_op jit(solution)/shard_map/reduce_scatter | solution.py:79
  256.3 206.5 %reduce-scatter.5.cloned.1.call-done = f32[256,128]{1,0:T(8,128)} async-done(((f32[4096,128]{1,0:T(8,128)}), f32[256,128]{1,0:T(8,128)}) %reduce-scatter.5.cloned.1.call-update) | async-done | bytes 131088 | tf_op jit(solution)/shard_map/reduce_scatter | solution.py:79
  462.8 1.6 add.43
  464.5 33.8 %all-reduce.3.cloned.1.call-done = f32[256,128]{1,0:T(8,128)} async-done(((f32[256,128]{1,0:T(8,128)}), f32[256,128]{1,0:T(8,128)}) %all-reduce.3.cloned.1.call-update) | async-done | bytes 131088 | tf_op jit(solution)/shard_map/psum | solution.py:82
  498.4 3.5 fusion.21
  501.9 219.1 %all-reduce.5.cloned.1.call-done = f32[2048,128]{1,0:T(8,128)} async-done(((f32[2048,128]{1,0:T(8,128)}), f32[2048,128]{1,0:T(8,128)}) %all-reduce.5.cloned.1.call-update) | async-done | bytes 1048592 | tf_op jit(solution)/shard_map/psum | solution.py:88
  721.0 2.3 broadcast_multiply_fusion
  (61 shorter events, 2.9 us)
Async XLA Ops:
  7.2 1.6 copy-start
  7.2 97.2 %all-gather.2.cloned.1.call-start = ((), (), s32[]{:S(2)}) async-start(), calls=%async_computation.2 | async-start | bytes 1114112 | tf_op jit(solution)/shard_map/all_gather | solution.py:42
  8.8 4.0 copy-start.5
  8.8 44.7 %copy-start.6 = (bf16[256,32]{0,1:T(8,128)(2,1)S(1)}, bf16[256,32]{0,1:T(8,128)(2,1)}, u32[]{:S(2)}) copy-start(bf16[256,32]{0,1:T(8,128)(2,1)} %param.10) | copy-start | bytes 49156
  10.1 43.5 %copy-start.2 = (bf16[256,2048]{1,0:T(8,128)(2,1)}, bf16[256,2048]{1,0:T(8,128)(2,1)S(1)}, u32[]{:S(2)}) copy-start(bf16[256,2048]{1,0:T(8,128)(2,1)S(1)} %gather_fusion) | copy-start | bytes 3145732
  12.7 243.6 %reduce-scatter.3.cloned.1.call-start = ((), (), s32[]{:S(2)}) async-start(), calls=%async_computation.3 | async-start | bytes 1179648 | tf_op jit(solution)/shard_map/reduce_scatter | solution.py:79
  104.4 2.7 copy-start.4
  109.8 1.3 copy-start.1
  116.7 2.7 copy-start.4
  122.2 1.3 copy-start.1
  129.4 2.7 copy-start.4
  134.8 1.3 copy-start.1
  142.1 2.7 copy-start.4
  147.5 1.3 copy-start.1
  154.8 2.7 copy-start.4
  160.2 1.3 copy-start.1
  167.4 2.7 copy-start.4
  172.9 1.3 copy-start.1
  180.1 2.7 copy-start.4
  185.6 1.3 copy-start.1
  192.8 2.7 copy-start.4
  198.2 1.3 copy-start.1
  208.0 254.8 %reduce-scatter.5.cloned.1.call-start = ((), (), s32[]{:S(2)}) async-start(), calls=%async_computation.4 | async-start | bytes 2228224 | tf_op jit(solution)/shard_map/reduce_scatter | solution.py:79
  208.8 289.6 %all-reduce.3.cloned.1.call-start = ((), (), s32[]{:S(2)}) async-start(), calls=%async_computation.5 | async-start | bytes 262144 | tf_op jit(solution)/shard_map/psum | solution.py:82
  464.5 256.5 %all-reduce.5.cloned.1.call-start = ((), (), s32[]{:S(2)}) async-start(), calls=%async_computation.6 | async-start | bytes 2097152 | tf_op jit(solution)/shard_map/psum | solution.py:88
  498.4 224.9 %copy-start.3 = (f32[256,128]{1,0:T(8,128)S(1)}, f32[256,128]{1,0:T(8,128)}, u32[]{:S(2)}) copy-start(f32[256,128]{1,0:T(8,128)} %all-reduce.3.cloned.1.call-done) | copy-start | bytes 393220
Sparse Core Ops, SparseCore 0:
  12.8 80.2 all-gather.1
  208.2 48.0 reduce-scatter.2
  260.2 202.5 reduce-scatter.4
  465.8 32.5 all-reduce.2
  504.1 216.8 all-reduce.4
where the time goes:
time: 735 us; the launch traced here: 730 us
  waiting for transfers between devices  508 us (69%)
  blocking collectives  89.7 us (12%)
  matrix products  88 us (12%)
  other arithmetic  16.8 us (2%)
  local copies, waits for them, and re-layouts  14 us (2%)
  between operations  13.9 us (2%)
    psum x1, waiting for transfers between devices, local(): head_grad = lax.psum(local_head, ('row', 'col')) * norm_factor  219 us
    reduce_scatter x1, waiting for transfers between devices, local(): lax.psum_scatter(col_part, 'row', scatter_dimension=0, tiled=True)  207 us
    reduce_scatter x1, waiting for transfers between devices, local(): lax.psum_scatter(row_part, 'col', scatter_dimension=0, tiled=True)  47.5 us
    all_gather x1, blocking collectives, local(): lax.all_gather(probe_right, 'row', axis=0, tiled=True)  39.4 us
    psum x1, waiting for transfers between devices, local(): embed_grad = lax.psum(owned, 'cores')  33.8 us
    dot_general x8, matrix products, tile_scattered(): jnp.dot(rounded_tile, block_embed, preferred_element_type=jnp.float32)  28.6 us
    all_gather x1, blocking collectives, local(): lax.all_gather(probe_left, 'col', axis=0, tiled=True)  26.3 us
    all_gather x1, blocking collectives, local(): lax.all_gather(embedding, 'col', axis=0, tiled=True)  24 us
  transfers between devices with their start and end apart: 5, of which 4 were waited for; matrix products, arithmetic and copies ran while one was open for 0% of the time, Pallas kernels for 0%

commit v1 on v0

v1 whole, which is shorter than its diff:
```python
import functools
import math

import jax
import jax.numpy as jnp
from jax import lax
from jax.experimental import pallas as pl
from jax.experimental.pallas import tpu as pltpu
from jax.sharding import PartitionSpec as P

MESH = pl.DeviceIdType.MESH
F32, BF16 = jnp.float32, jnp.bfloat16
NX, NY, NZ = 4, 4, 8
PLANE = NX * NY


def dot(a, b, ca, cb):
    return lax.dot_general(a, b, (((ca,), (cb,)), ((), ())), preferred_element_type=F32)


def squares(z):
    zf = z.astype(F32)
    sq = zf * zf
    hi = sq.astype(BF16)
    return hi, (sq - hi.astype(F32)).astype(BF16)


def fused(norm, idx_ref, feat_hbm, w_hbm, left_ref, right_ref, head_out, embed_out,
          feat, w, e_all, ft, u_buf, u_in, z_own, zA, lrA, qA, zB, rlB, qB, acc, mass,
          gs, gr, gfull, hp, hr, hz, hb,
          feat_sem, w_sem, u_sem, az_s, az_r, al_s, al_r, fz_s, fz_r, fl_s, fl_r,
          bz_s, bz_r, bl_s, bl_r, g_s, g_r, gx_sem, hr_s, hr_r, hz_s, hz_r, ha_s, ha_r, hf_s, hf_r):
    row, col, core = lax.axis_index("row"), lax.axis_index("col"), lax.axis_index("cores")
    x, y, z = (row // NZ) * 2 + col // NY, col % NY, row % NZ
    half = z_own.shape[1]
    embed = z_own.shape[2]
    scale = 0.5 / embed * math.log2(math.e)

    def at(dx, dy, dz, dc):
        nx, ny, nz = (x + dx) % NX, (y + dy) % NY, (z + dz) % NZ
        return ((nx // 2) * NZ + nz, (nx % 2) * NY + ny, (core + dc) % 2)

    def plane_at(n):
        return at(n // NY, n % NY, 0, 0)

    def remote(src, dst, ssem, rsem, device):
        return pltpu.make_async_remote_copy(
            src_ref=src, dst_ref=dst, send_sem=ssem, recv_sem=rsem, device_id=device, device_id_type=MESH)

    sibling = at(0, 0, 0, 1)
    me_plane = x * NY + y
    other = 1 - core

    chunk = feat.shape[0] // 4
    w_copy = pltpu.make_async_copy(w_hbm, w, w_sem)
    w_copy.start()
    feat_copies = [
        pltpu.make_async_copy(feat_hbm.at[pl.ds(i * chunk, chunk)], feat.at[pl.ds(i * chunk, chunk)], feat_sem.at[i])
        for i in range(4)]
    for c in feat_copies:
        c.start()

    barrier = pltpu.get_barrier_semaphore()
    for n in range(1, PLANE):
        pl.semaphore_signal(barrier, inc=1, device_id=plane_at(n), device_id_type=MESH)
    for j in range(1, NZ):
        pl.semaphore_signal(barrier, inc=1, device_id=at(0, 0, j, 0), device_id_type=MESH)
    pl.semaphore_signal(barrier, inc=1, device_id=sibling, device_id_type=MESH)

    probes = left_ref.shape[1]
    lane = lax.broadcasted_iota(jnp.int32, (probes, embed), 1)
    sub = lax.broadcasted_iota(jnp.int32, (probes, embed), 0)
    first = (lane == sub + 2 * probes * core).astype(F32).astype(BF16)
    second = (lane == sub + 2 * probes * core + probes).astype(F32).astype(BF16)
    lv, rv = left_ref[...], right_ref[...]
    u = (dot(lv, first, 1, 0) + dot(rv, second, 1, 0)).astype(BF16)
    v = (dot(lv, second, 1, 0) + dot(rv, first, 1, 0)).astype(BF16)
    for h in range(2):
        u_buf[h, 0] = u[h * half:(h + 1) * half]
        u_buf[h, 1] = v[h * half:(h + 1) * half]

    w_copy.wait()
    for i, c in enumerate(feat_copies):
        c.wait()
        e_all[pl.ds(i * chunk, chunk)] = dot(feat[pl.ds(i * chunk, chunk)], w[...], 1, 0).astype(BF16)
    index = idx_ref[...].reshape(1, 2 * half)
    onehot = (lax.broadcasted_iota(jnp.int32, (feat.shape[0], 2 * half), 0) == index).astype(F32).astype(BF16)
    z_all = dot(onehot, e_all[...], 0, 0).astype(BF16)
    z_own[0] = z_all[:half]
    z_own[1] = z_all[half:]
    mine = z_own[core]
    zA[0, 0] = mine
    zA[1, 0] = z_own[other]
    zB[0] = mine

    pl.semaphore_wait(barrier, PLANE - 1 + NZ - 1 + 1)

    u_copy = remote(u_buf.at[other], u_in, u_sem.at[0], u_sem.at[1], sibling)
    u_copy.start()
    za_copies = [None] + [remote(zA.at[0, 0], zA.at[0, n], az_s.at[n], az_r.at[n], plane_at(n)) for n in range(1, PLANE)]
    zb_copies = [None] + [remote(zB.at[0], zB.at[j], bz_s.at[j], bz_r.at[j], at(0, 0, j, 0)) for j in range(1, NZ)]
    for n in range(1, PLANE):
        za_copies[n].start()
        if n < NZ:
            zb_copies[n].start()
    u_copy.wait_recv()
    lrA[0, 0] = u_buf[core, 0] + u_in[0]
    rlB[0] = u_buf[core, 1] + u_in[1]
    la_copies = [None] + [remote(lrA.at[0, 0], lrA.at[0, n], al_s.at[n], al_r.at[n], plane_at(n)) for n in range(1, PLANE)]
    lb_copies = [None] + [remote(rlB.at[0], rlB.at[j], bl_s.at[j], bl_r.at[j], at(0, 0, j, 0)) for j in range(1, NZ)]
    for n in range(1, PLANE):
        la_copies[n].start()
        if n < NZ:
            lb_copies[n].start()
    fl_copies = [remote(lrA.at[0, n], lrA.at[1, n], fl_s.at[n], fl_r.at[n], sibling) for n in range(PLANE)]
    fz_copies = [None] + [remote(zA.at[0, n], zA.at[1, n], fz_s.at[n], fz_r.at[n], sibling) for n in range(1, PLANE)]
    fl_copies[0].start()

    columns = feat.shape[1] // 2
    ft[...] = dot(feat[:, pl.ds(pl.multiple_of(core * columns, columns), columns)], onehot, 0, 0).astype(BF16)
    acc[...] = jnp.zeros_like(acc)
    mass[...] = jnp.zeros_like(mass)
    ones = jnp.ones((8, embed), BF16)

    def norms_a(h, n):
        hi, lo = squares(zA[h, n])
        qA[h, n] = (dot(ones, hi, 1, 1) + dot(ones, lo, 1, 1)) * scale

    def norms_b(j):
        hi, lo = squares(zB[j])
        wide = jnp.ones((embed, embed), BF16)
        qB[j] = (dot(hi, wide, 1, 0) + dot(lo, wide, 1, 0)) * scale

    norms_a(0, 0)
    norms_a(1, 0)
    norms_b(0)
    for n in range(1, PLANE):
        za_copies[n].wait_recv()
        fz_copies[n].start()
        norms_a(0, n)
        if n < NZ:
            zb_copies[n].wait_recv()
            norms_b(n)
    for j in range(1, NZ):
        lb_copies[j].wait_recv()

    def tile(h, m, j, blocks):
        rows = blocks * half
        zb = zB[pl.ds(j, blocks)].reshape(rows, embed)
        rl = rlB[pl.ds(j, blocks)].reshape(rows, embed)
        qb = qB[pl.ds(j, blocks)].reshape(rows, embed)
        za = zA[h, pl.ds(2 * m, 2)].reshape(2 * half, embed)
        lr = lrA[h, pl.ds(2 * m, 2)].reshape(2 * half, embed)
        qa = jnp.concatenate([qA[h, 2 * m, 0:1], qA[h, 2 * m + 1, 0:1]], axis=1)
        products = dot(zb, za, 1, 1)
        pairs = dot(rl, lr, 1, 1)
        weight = jnp.exp2(products * (2.0 * scale) - (jnp.concatenate([qb, qb], axis=1) + qa)) * pairs
        part = dot(weight.astype(BF16), za, 1, 0)
        acc[pl.ds(j, blocks)] += part.reshape(blocks, half, embed)
        mass[pl.ds(j, blocks)] += (weight[:, :half] + weight[:, half:]).reshape(blocks, half, embed)

    def first_half(m, carry):
        for n in (2 * m, 2 * m + 1):
            @pl.when(n > 0)
            def _():
                remote(lrA.at[0, 0], lrA.at[0, n], al_s.at[n], al_r.at[n], sibling).wait_recv()
                remote(lrA.at[0, n], lrA.at[1, n], fl_s.at[n], fl_r.at[n], sibling).start()
        for j in range(0, NZ, 2):
            tile(0, m, j, 2)
        return carry

    lax.fori_loop(0, PLANE // 2, first_half, 0)

    for n in range(1, PLANE):
        fz_copies[n].wait_recv()
        norms_a(1, n)
    for n in range(PLANE):
        fl_copies[n].wait_recv()

    g_copies = [None] + [remote(gs.at[j], gr.at[j], g_s.at[j], g_r.at[j], at(0, 0, NZ - j, 0)) for j in range(1, NZ)]
    for j in (4, 2, 6, 0):
        def second_half(m, carry, j=j):
            tile(1, m, j, 2)
            return carry

        lax.fori_loop(0, PLANE // 2, second_half, 0)
        for i in (j, j + 1):
            total = jnp.sum(mass[i], axis=1, keepdims=True)
            grad = (acc[i] - total * zB[i].astype(F32)) * (1.0 / embed)
            if i == 0:
                acc[0] = grad
            else:
                gs[i] = grad.astype(BF16)
                g_copies[i].start()

    for n in range(1, PLANE):
        za_copies[n].wait_send()
        la_copies[n].wait_send()
        fz_copies[n].wait_send()
    for n in range(PLANE):
        fl_copies[n].wait_send()
    for j in range(1, NZ):
        zb_copies[j].wait_send()
        lb_copies[j].wait_send()
    u_copy.wait_send()

    grad = acc[0]
    for j in range(1, NZ):
        g_copies[j].wait_recv()
        grad = grad + gr[j].astype(F32)
    gfull[core] = grad
    gx = remote(gfull.at[core], gfull.at[core], gx_sem.at[0], gx_sem.at[1], sibling)
    gx.start()
    for j in range(1, NZ):
        g_copies[j].wait_send()
    gx.wait()

    both = gfull[...].reshape(2 * half, embed)
    embed_out[...] = both
    hi = both.astype(BF16)
    lo = (both - hi.astype(F32)).astype(BF16)
    wide = dot(ft[...], jnp.concatenate([hi, lo], axis=1), 1, 0)
    hp[...] = (wide[:, :embed] + wide[:, embed:]).astype(BF16).reshape(hp.shape)

    def slice_of(n):
        return ((x + n // NY) % NX) * NY + (y + n % NY) % NY

    hr_copies = [None] + [remote(hp.at[slice_of(n)], hr.at[n], hr_s.at[n], hr_r.at[n], plane_at(n)) for n in range(1, PLANE)]
    for n in range(1, PLANE):
        hr_copies[n].start()
    total = hp[me_plane].astype(F32)
    for n in range(1, PLANE):
        hr_copies[n].wait_recv()
        total = total + hr[n].astype(F32)
    hz[z] = (total * norm).astype(BF16)

    hz_copies = [None] + [remote(hz.at[z], hz.at[z], hz_s.at[j], hz_r.at[j], at(0, 0, j, 0)) for j in range(1, NZ)]
    for j in range(1, NZ):
        hz_copies[j].start()
    for n in range(1, PLANE):
        hr_copies[n].wait_send()
    for j in range(1, NZ):
        hz_copies[j].wait_recv()
    total = hz[0].astype(F32)
    for j in range(1, NZ):
        total = total + hz[j].astype(F32)
    hb[core, me_plane] = total.astype(BF16)

    ha_copies = [None] + [
        remote(hb.at[core, me_plane], hb.at[core, me_plane], ha_s.at[n], ha_r.at[n], plane_at(n)) for n in range(1, PLANE)]
    for n in range(1, PLANE):
        ha_copies[n].start()
    hf_copies = []
    for n in range(PLANE):
        source = ((x + NX - n // NY) % NX) * NY + (y + NY - n % NY) % NY
        if n:
            ha_copies[n].wait_recv()
        c = remote(hb.at[core, source], hb.at[core, source], hf_s.at[n], hf_r.at[n], sibling)
        c.start()
        hf_copies.append(c)
    for j in range(1, NZ):
        hz_copies[j].wait_send()
    for n in range(1, PLANE):
        ha_copies[n].wait_send()
    for c in hf_copies:
        c.wait()
    head_out[...] = hb[...].reshape(head_out.shape)


def finish(head_in, embed_in, embed_out, head_out):
    embed_out[...] = embed_in[...]
    head_out[...] = head_in[...].astype(F32)


def local(batch_index, chip_features, head_weight, probe_left, probe_right):
    points = batch_index.shape[0]
    half = points // 2
    chips, width = chip_features.shape
    embed = head_weight.shape[1]
    rows = width // 2 // PLANE
    norm = 1.0 / math.sqrt(points * PLANE * NZ)
    block = (half, embed)
    vmem, dma = pltpu.VMEM, pltpu.SemaphoreType.DMA
    head, grad = pl.pallas_call(
        functools.partial(fused, norm),
        out_shape=(jax.ShapeDtypeStruct((width, embed), BF16), jax.ShapeDtypeStruct((points, embed), F32)),
        in_specs=[pl.BlockSpec(memory_space=pltpu.VMEM), pl.BlockSpec(memory_space=pl.ANY),
                  pl.BlockSpec(memory_space=pl.ANY), pl.BlockSpec(memory_space=pltpu.VMEM),
                  pl.BlockSpec(memory_space=pltpu.VMEM)],
        out_specs=[pl.BlockSpec(memory_space=pltpu.VMEM)] * 2,
        scratch_shapes=[
            vmem((chips, width), BF16), vmem((width, embed), BF16), vmem((chips, embed), BF16),
            vmem((width // 2, points), BF16), vmem((2, 2) + block, BF16), vmem((2,) + block, BF16),
            vmem((2,) + block, BF16), vmem((2, PLANE) + block, BF16), vmem((2, PLANE) + block, BF16),
            vmem((2, PLANE, 8, half), F32), vmem((NZ,) + block, BF16), vmem((NZ,) + block, BF16),
            vmem((NZ,) + block, F32), vmem((NZ,) + block, F32), vmem((NZ,) + block, F32),
            vmem((NZ,) + block, BF16), vmem((NZ,) + block, BF16), vmem((2,) + block, F32),
            vmem((PLANE, rows, embed), BF16), vmem((PLANE, rows, embed), BF16),
            vmem((NZ, rows, embed), BF16), vmem((2, PLANE, rows, embed), BF16),
            dma((4,)), dma, dma((2,)),
            dma((PLANE,)), dma((PLANE,)), dma((PLANE,)), dma((PLANE,)),
            dma((PLANE,)), dma((PLANE,)), dma((PLANE,)), dma((PLANE,)),
            dma((NZ,)), dma((NZ,)), dma((NZ,)), dma((NZ,)), dma((NZ,)), dma((NZ,)), dma((2,)),
            dma((PLANE,)), dma((PLANE,)), dma((NZ,)), dma((NZ,)),
            dma((PLANE,)), dma((PLANE,)), dma((PLANE,)), dma((PLANE,)),
        ],
        compiler_params=pltpu.CompilerParams(
            collective_id=0, has_side_effects=True, vmem_limit_bytes=48 * 2**20),
    )(batch_index, chip_features, head_weight, probe_left, probe_right)
    return pl.pallas_call(
        finish,
        out_shape=(jax.ShapeDtypeStruct((points, embed), F32), jax.ShapeDtypeStruct((width, embed), F32)),
        in_specs=[pl.BlockSpec(memory_space=pltpu.VMEM)] * 2,
        out_specs=[pl.BlockSpec(memory_space=pltpu.VMEM)] * 2,
    )(head, grad)


def solution(mesh):
    return jax.shard_map(
        local,
        mesh=mesh,
        in_specs=(P(("row", "col")), P(("row", "col"), None), P(), P(("row", "col"), "cores"), P(("row", "col"), "cores")),
        out_specs=(P(("row", "col"), None), P()),
        check_vma=False,
    )
```

time: 735 us -> 84 us (0.11)
  waiting for transfers between devices: 508 us -> 0 us
  blocking collectives: 89.7 us -> 0 us
  matrix products: 88 us -> 0 us
  Pallas kernels: 0 us -> 76.7 us
  other arithmetic: 16.8 us -> 0 us
  between operations: 13.9 us -> 0.66 us
  local copies, waits for them, and re-layouts: 14 us -> 6.41 us
    reduce_scatter x2 -> x0, waiting for transfers between devices: 254 us -> none  [the longest x1 207 us: local(): lax.psum_scatter(col_part, 'row', scatter_dimension=0, tiled=True)]
    psum x2 -> x0, waiting for transfers between devices: 253 us -> none  [the longest x1 219 us: local(): head_grad = lax.psum(local_head, ('row', 'col')) * norm_factor]
    all_gather x3 -> x0, blocking collectives: 89.7 us -> none  [the longest x1 39.4 us: local(): lax.all_gather(probe_right, 'row', axis=0, tiled=True)]
    dot_general x34 -> x0, matrix products: 88 us -> none  [the longest x8 28.6 us: tile_scattered(): jnp.dot(rounded_tile, block_embed, preferred_element_type=jnp.float32)]
    pallas_call x0 -> x2, Pallas kernels: none -> 76.7 us  [the longest x1 74.6 us: local(): pl.pallas_call(functools.partial(fused, norm), out_shape=(jax.ShapeDtypeS...]
    while x32 -> x0, local copies, waits for them, and re-layouts: 10.5 us -> none
    reduce_sum x9 -> x0, other arithmetic: 8.79 us -> none  [the longest x8 8.44 us: kernel_block(): col_square = jnp.sum(col_float * col_float, axis=1)]
  transfers between devices with their start and end apart: 5 -> 0, of which waited for: 4 -> 0; matrix products, arithmetic and copies ran while one was open for 0% -> 0% of each run, Pallas kernels for 0% -> 0%
where the time goes in v1:
time: 84 us; the launch traced here: 83.7 us
  Pallas kernels  76.7 us (91%)
  local copies, waits for them, and re-layouts  6.41 us (8%)
    pallas_call x1, Pallas kernels, local(): pl.pallas_call(functools.partial(fused, norm), out_shape=(jax.ShapeDtypeS...  74.6 us
    unnamed x12, local copies, waits for them, and re-layouts  6.41 us
    pallas_call x1, Pallas kernels, local(): pl.pallas_call(finish, out_shape=(jax.ShapeDtypeStruct((points, embed), F...  2.11 us

profile of v1, /device:TPU:1, one launch (start us, length us, event | category | flops | bytes accessed | tf_op | source)
XLA Modules:
  0.0 83.7 jit_solution(5872827025472221800)
XLA Ops:
  0.6 0.8 copy.7.left_ref
  1.5 0.8 %copy.8.right_ref = bf16[256,32]{1,0:T(8,128)(2,1)S(1)} copy(bf16[256,32]{0,1:T(8,128)(2,1)} %param.9) | data formatting | bytes 32768 | tf_op args[4]
  2.3 0.0 copy-start
  2.3 1.6 %copy-done = bf16[512,2048]{1,0:T(8,128)(2,1)S(1)} copy-done((bf16[512,2048]{1,0:T(8,128)(2,1)S(1)}, bf16[512,2048]{1,0:T(8,128)(2,1)}, u32[]{:S(2)}) %copy-start) | copy-done | bytes 2097176
  3.9 0.0 copy-start.1
  3.9 1.0 %copy-done.1 = bf16[2048,128]{1,0:T(8,128)(2,1)S(1)} copy-done((bf16[2048,128]{1,0:T(8,128)(2,1)S(1)}, bf16[2048,128]{1,0:T(8,128)(2,1)}, u32[]{:S(2)}) %copy-start.1) | copy-done | bytes 524312
  4.9 0.0 copy-start.4
  4.9 0.7 copy-done.4
  5.6 74.6 %shard_map.68 = (bf16[2048,128]{1,0:T(8,128)(2,1)S(1)}, f32[256,128]{1,0:T(8,128)S(1)}) custom-call(s32[256]{0:T(256)S(1)} %copy-done.4, bf16[512,2048]{1,0:T(8,128)(2,1)S(1)} %copy-done, bf16[2048,128]{1,0:T(8,128)(2,1)S(1)} %copy-done.1, bf16[256,32]{1,0:T(8,128)(2,1)S(1)} %copy.7.left_ref, bf16[256,32]{1,0:T(8,128)(2,1)S(1)} %copy.8.right_ref), custom_call_target="tpu_custom_call" | custom-call | tf_op jit(solution)/shard_map/pallas_call | solution.py:284
  80.2 0.0 copy-start.2
  80.2 0.8 copy-done.2
  81.0 0.0 copy-start.3
  81.0 0.6 copy-done.3
  81.6 2.1 %shard_map.69 = (f32[256,128]{1,0:T(8,128)}, f32[2048,128]{1,0:T(8,128)}) custom-call(bf16[2048,128]{1,0:T(8,128)(2,1)} %copy-done.2, f32[256,128]{1,0:T(8,128)} %copy-done.3), custom_call_target="tpu_custom_call" | custom-call | tf_op jit(solution)/shard_map/pallas_call | solution.py:310
Async XLA Ops:
  2.3 1.6 %copy-start = (bf16[512,2048]{1,0:T(8,128)(2,1)S(1)}, bf16[512,2048]{1,0:T(8,128)(2,1)}, u32[]{:S(2)}) copy-start(bf16[512,2048]{1,0:T(8,128)(2,1)} %feat_hbm.1) | copy-start | bytes 6291460
  3.9 1.0 %copy-start.1 = (bf16[2048,128]{1,0:T(8,128)(2,1)S(1)}, bf16[2048,128]{1,0:T(8,128)(2,1)}, u32[]{:S(2)}) copy-start(bf16[2048,128]{1,0:T(8,128)(2,1)} %w_hbm.1) | copy-start | bytes 1572868
  4.9 0.7 copy-start.4
  80.2 0.8 copy-start.2
  81.0 0.6 copy-start.3

commit v2 on v1

v2 whole, which is shorter than its diff:
```python
import functools
import math

import jax
import jax.numpy as jnp
from jax import lax
from jax.experimental import pallas as pl
from jax.experimental.pallas import tpu as pltpu
from jax.sharding import PartitionSpec as P

MESH = pl.DeviceIdType.MESH
F32, BF16 = jnp.float32, jnp.bfloat16
NX, NY, NZ = 4, 4, 8
PLANE = NX * NY


def dot(a, b, ca, cb):
    return lax.dot_general(a, b, (((ca,), (cb,)), ((), ())), preferred_element_type=F32)


def squares(z):
    zf = z.astype(F32)
    sq = zf * zf
    hi = sq.astype(BF16)
    return hi, (sq - hi.astype(F32)).astype(BF16)


def fused(norm, idx_hbm, feat_hbm, w_hbm, left_hbm, right_hbm, head_out, embed_out,
          idx_ref, left_ref, right_ref, feat, w, e_all, ft, u_buf, u_in, z_own, zA, lrA, qA, zB, rlB, qB, acc, mass,
          gs, gr, gfull, hp, hr, hz, hb,
          feat_sem, in_sem, u_sem, az_s, az_r, al_s, al_r, fz_s, fz_r, fl_s, fl_r,
          bz_s, bz_r, bl_s, bl_r, g_s, g_r, gx_sem, hr_s, hr_r, hz_s, hz_r, ha_s, ha_r, hf_s, hf_r):
    row, col, core = lax.axis_index("row"), lax.axis_index("col"), lax.axis_index("cores")
    x, y, z = (row // NZ) * 2 + col // NY, col % NY, row % NZ
    half = z_own.shape[1]
    embed = z_own.shape[2]
    scale = 0.5 / embed * math.log2(math.e)

    def at(dx, dy, dz, dc):
        nx, ny, nz = (x + dx) % NX, (y + dy) % NY, (z + dz) % NZ
        return ((nx // 2) * NZ + nz, (nx % 2) * NY + ny, (core + dc) % 2)

    def plane_at(n):
        return at(n // NY, n % NY, 0, 0)

    def remote(src, dst, ssem, rsem, device):
        return pltpu.make_async_remote_copy(
            src_ref=src, dst_ref=dst, send_sem=ssem, recv_sem=rsem, device_id=device, device_id_type=MESH)

    sibling = at(0, 0, 0, 1)
    me_plane = x * NY + y
    other = 1 - core

    chunk = feat.shape[0] // 4
    small_copies = [
        pltpu.make_async_copy(src, dst, in_sem.at[i])
        for i, (src, dst) in enumerate(((left_hbm, left_ref), (right_hbm, right_ref), (idx_hbm, idx_ref), (w_hbm, w)))]
    for c in small_copies:
        c.start()
    feat_copies = [
        pltpu.make_async_copy(feat_hbm.at[pl.ds(i * chunk, chunk)], feat.at[pl.ds(i * chunk, chunk)], feat_sem.at[i])
        for i in range(4)]
    for c in feat_copies:
        c.start()

    barrier = pltpu.get_barrier_semaphore()
    for n in range(1, PLANE):
        pl.semaphore_signal(barrier, inc=1, device_id=plane_at(n), device_id_type=MESH)
    for j in range(1, NZ):
        pl.semaphore_signal(barrier, inc=1, device_id=at(0, 0, j, 0), device_id_type=MESH)
    pl.semaphore_signal(barrier, inc=1, device_id=sibling, device_id_type=MESH)

    probes = left_ref.shape[0]
    lane = lax.broadcasted_iota(jnp.int32, (probes, embed), 1)
    sub = lax.broadcasted_iota(jnp.int32, (probes, embed), 0)
    first = (lane == sub + 2 * probes * core).astype(F32).astype(BF16)
    second = (lane == sub + 2 * probes * core + probes).astype(F32).astype(BF16)
    small_copies[0].wait()
    small_copies[1].wait()
    lv, rv = left_ref[...], right_ref[...]
    u = (dot(lv, first, 0, 0) + dot(rv, second, 0, 0)).astype(BF16)
    v = (dot(lv, second, 0, 0) + dot(rv, first, 0, 0)).astype(BF16)
    for h in range(2):
        u_buf[h, 0] = u[h * half:(h + 1) * half]
        u_buf[h, 1] = v[h * half:(h + 1) * half]

    small_copies[3].wait()
    for i, c in enumerate(feat_copies):
        c.wait()
        e_all[pl.ds(i * chunk, chunk)] = dot(feat[pl.ds(i * chunk, chunk)], w[...], 1, 0).astype(BF16)
    small_copies[2].wait()
    index = idx_ref[...].reshape(1, 2 * half)
    onehot = (lax.broadcasted_iota(jnp.int32, (feat.shape[0], 2 * half), 0) == index).astype(F32).astype(BF16)
    z_all = dot(onehot, e_all[...], 0, 0).astype(BF16)
    z_own[0] = z_all[:half]
    z_own[1] = z_all[half:]
    mine = z_own[core]
    zA[0, 0] = mine
    zA[1, 0] = z_own[other]
    zB[0] = mine

    pl.semaphore_wait(barrier, PLANE - 1 + NZ - 1 + 1)

    sends = []

    def send(src, dst, ssem, rsem, device):
        c = remote(src, dst, ssem, rsem, device)
        c.start()
        sends.append(c)
        return c

    def send_z(n, m):
        d = m - n
        return send(zA.at[0, n], zA.at[0, m], az_s.at[m], az_r.at[m], plane_at(d))

    def send_l(n, m):
        return send(lrA.at[0, n], lrA.at[0, m], al_s.at[m], al_r.at[m], plane_at(m - n))

    def line_z(i, j):
        return send(zB.at[i], zB.at[j], bz_s.at[j], bz_r.at[j], at(0, 0, (j - i) % NZ, 0))

    def line_l(i, j):
        return send(rlB.at[i], rlB.at[j], bl_s.at[j], bl_r.at[j], at(0, 0, (j - i) % NZ, 0))

    def arrived(buf, sems):
        remote(buf, buf, sems, sems, sibling).wait_recv()

    u_copy = send(u_buf.at[other], u_in, u_sem.at[0], u_sem.at[1], sibling)
    near = (1, 3, 2)
    for d in near:
        send_z(0, NY * d)
    line_z(0, 2)
    line_z(0, 6)
    for d in near:
        send_z(0, d)
    line_z(0, 1)
    line_z(0, 7)
    u_copy.wait_recv()
    lrA[0, 0] = u_buf[core, 0] + u_in[0]
    rlB[0] = u_buf[core, 1] + u_in[1]
    for d in near:
        send_l(0, d)
    line_l(0, 2)
    line_l(0, 6)
    for d in near:
        send_l(0, NY * d)
    line_l(0, 1)
    line_l(0, 7)

    def forward_z(n):
        return remote(zA.at[0, n], zA.at[1, n], fz_s.at[n], fz_r.at[n], sibling)

    def forward_l(n):
        return remote(lrA.at[0, n], lrA.at[1, n], fl_s.at[n], fl_r.at[n], sibling)

    forward_l(0).start()
    ones = jnp.ones((8, embed), BF16)

    def norms_a(h, n):
        hi, lo = squares(zA[h, n])
        qA[h, n] = (dot(ones, hi, 1, 1) + dot(ones, lo, 1, 1)) * scale

    def norms_b(j):
        hi, lo = squares(zB[j])
        wide = jnp.ones((embed, embed), BF16)
        qB[j] = (dot(hi, wide, 1, 0) + dot(lo, wide, 1, 0)) * scale

    for d in near:
        arrived(zA.at[0, NY * d], az_r.at[NY * d])
        for e in near:
            send_z(NY * d, NY * d + e)
    arrived(zB.at[2], bz_r.at[2])
    line_z(2, 3)
    line_z(2, 4)
    arrived(zB.at[6], bz_r.at[6])
    line_z(6, 5)
    for d in near:
        arrived(lrA.at[0, d], al_r.at[d])
        for e in near:
            send_l(d, NY * e + d)
    arrived(rlB.at[2], bl_r.at[2])
    line_l(2, 3)
    arrived(rlB.at[6], bl_r.at[6])
    line_l(6, 5)
    line_l(6, 4)

    columns = feat.shape[1] // 2
    ft[...] = dot(feat[:, pl.ds(pl.multiple_of(core * columns, columns), columns)], onehot, 0, 0).astype(BF16)
    acc[...] = jnp.zeros_like(acc)
    mass[...] = jnp.zeros_like(mass)
    norms_a(0, 0)
    norms_a(1, 0)
    for d in near:
        forward_z(NY * d).start()
        norms_a(0, NY * d)
    for j in (0, 2, 6, 1, 7, 3, 5, 4):
        if j in (1, 3, 4, 5, 7):
            arrived(zB.at[j], bz_r.at[j])
        norms_b(j)
    for j in (1, 7, 3, 5, 4):
        arrived(rlB.at[j], bl_r.at[j])

    def tile(h, n, count, j, blocks):
        rows = blocks * half
        zb = zB[pl.ds(j, blocks)].reshape(rows, embed)
        rl = rlB[pl.ds(j, blocks)].reshape(rows, embed)
        qb = qB[pl.ds(j, blocks)].reshape(rows, embed)
        za = zA[h, pl.ds(n, count)].reshape(count * half, embed)
        lr = lrA[h, pl.ds(n, count)].reshape(count * half, embed)
        qa = jnp.concatenate([qA[h, n + i, 0:1] for i in range(count)], axis=1)
        products = dot(zb, za, 1, 1)
        pairs = dot(rl, lr, 1, 1)
        weight = jnp.exp2(products * (2.0 * scale) - (jnp.concatenate([qb] * count, axis=1) + qa)) * pairs
        part = dot(weight.astype(BF16), za, 1, 0)
        acc[pl.ds(j, blocks)] += part.reshape(blocks, half, embed)
        row_mass = weight[:, :half]
        for i in range(1, count):
            row_mass = row_mass + weight[:, i * half:(i + 1) * half]
        mass[pl.ds(j, blocks)] += row_mass.reshape(blocks, half, embed)

    for d in (0, 1, 3, 2):
        for e in (0, 1, 3, 2):
            n = NY * d + e
            if e:
                arrived(zA.at[0, n], az_r.at[n])
                forward_z(n).start()
                norms_a(0, n)
            if n and not (d == 0):
                arrived(lrA.at[0, n], al_r.at[n])
            if n:
                forward_l(n).start()
        tile(0, NY * d, NY, 0, NZ)

    for n in range(1, PLANE):
        arrived(zA.at[1, n], fz_r.at[n])
        norms_a(1, n)
    for n in range(PLANE):
        arrived(lrA.at[1, n], fl_r.at[n])

    g_copies = [None] + [remote(gs.at[j], gr.at[j], g_s.at[j], g_r.at[j], at(0, 0, NZ - j, 0)) for j in range(1, NZ)]
    for j in (4, 2, 6, 0):
        tile(1, 0, PLANE, j, 2)
        for i in (j + 1, j):
            total = jnp.sum(mass[i], axis=1, keepdims=True)
            grad = (acc[i] - total * zB[i].astype(F32)) * (1.0 / embed)
            if i == 0:
                acc[0] = grad
            else:
                gs[i] = grad.astype(BF16)
                g_copies[i].start()

    for c in sends:
        c.wait_send()
    for n in range(PLANE):
        if n:
            forward_z(n).wait_send()
        forward_l(n).wait_send()

    grad = acc[0]
    for j in range(1, NZ):
        g_copies[j].wait_recv()
        grad = grad + gr[j].astype(F32)
    gfull[core] = grad
    gx = remote(gfull.at[core], gfull.at[core], gx_sem.at[0], gx_sem.at[1], sibling)
    gx.start()
    for j in range(1, NZ):
        g_copies[j].wait_send()
    gx.wait()

    both = gfull[...].reshape(2 * half, embed)
    embed_out[...] = both
    hi = both.astype(BF16)
    lo = (both - hi.astype(F32)).astype(BF16)
    wide = dot(ft[...], jnp.concatenate([hi, lo], axis=1), 1, 0)
    hp[...] = (wide[:, :embed] + wide[:, embed:]).astype(BF16).reshape(hp.shape)

    def slice_of(n):
        return ((x + n // NY) % NX) * NY + (y + n % NY) % NY

    hr_copies = [None] + [remote(hp.at[slice_of(n)], hr.at[n], hr_s.at[n], hr_r.at[n], plane_at(n)) for n in range(1, PLANE)]
    for n in range(1, PLANE):
        hr_copies[n].start()
    total = hp[me_plane].astype(F32)
    for n in range(1, PLANE):
        hr_copies[n].wait_recv()
        total = total + hr[n].astype(F32)
    hz[z] = (total * norm).astype(BF16)

    hz_copies = [None] + [remote(hz.at[z], hz.at[z], hz_s.at[j], hz_r.at[j], at(0, 0, j, 0)) for j in range(1, NZ)]
    for j in range(1, NZ):
        hz_copies[j].start()
    for n in range(1, PLANE):
        hr_copies[n].wait_send()
    for j in range(1, NZ):
        hz_copies[j].wait_recv()
    total = hz[0].astype(F32)
    for j in range(1, NZ):
        total = total + hz[j].astype(F32)
    hb[core, me_plane] = total.astype(BF16)

    ha_copies = [None] + [
        remote(hb.at[core, me_plane], hb.at[core, me_plane], ha_s.at[n], ha_r.at[n], plane_at(n)) for n in range(1, PLANE)]
    by_distance = sorted(range(PLANE), key=lambda n: min(n // NY, NX - n // NY) + min(n % NY, NY - n % NY))
    for n in by_distance[:0:-1]:
        ha_copies[n].start()
    hf_copies = []
    for n in by_distance:
        source = ((x + NX - n // NY) % NX) * NY + (y + NY - n % NY) % NY
        if n:
            ha_copies[n].wait_recv()
        c = remote(hb.at[core, source], hb.at[core, source], hf_s.at[n], hf_r.at[n], sibling)
        c.start()
        hf_copies.append(c)
    for j in range(1, NZ):
        hz_copies[j].wait_send()
    for n in range(1, PLANE):
        ha_copies[n].wait_send()
    for c in hf_copies:
        c.wait()
    head_out[...] = hb[...].reshape(head_out.shape)


def finish(head_in, embed_in, embed_out, head_out, head_v, head_f, embed_v, in_sem, out_sem):
    pieces = in_sem.shape[0] - 1
    rows = head_v.shape[0] // pieces
    cuts = [pl.ds(i * rows, rows) for i in range(pieces)]
    ins = [pltpu.make_async_copy(head_in.at[cut], head_v.at[cut], in_sem.at[i]) for i, cut in enumerate(cuts)]
    outs = [pltpu.make_async_copy(head_f.at[cut], head_out.at[cut], out_sem.at[i]) for i, cut in enumerate(cuts)]
    embed_load = pltpu.make_async_copy(embed_in, embed_v, in_sem.at[pieces])
    embed_store = pltpu.make_async_copy(embed_v, embed_out, out_sem.at[pieces])
    for c in ins:
        c.start()
    embed_load.start()
    for i, cut in enumerate(cuts):
        ins[i].wait()
        head_f[cut] = head_v[cut].astype(F32)
        outs[i].start()
    embed_load.wait()
    embed_store.start()
    for c in outs:
        c.wait()
    embed_store.wait()


def local(batch_index, chip_features, head_weight, probe_left, probe_right):
    points = batch_index.shape[0]
    half = points // 2
    chips, width = chip_features.shape
    probes = probe_left.shape[1]
    embed = head_weight.shape[1]
    rows = width // 2 // PLANE
    norm = 1.0 / math.sqrt(points * PLANE * NZ)
    block = (half, embed)
    vmem, dma = pltpu.VMEM, pltpu.SemaphoreType.DMA
    head, grad = pl.pallas_call(
        functools.partial(fused, norm),
        out_shape=(jax.ShapeDtypeStruct((width, embed), BF16), jax.ShapeDtypeStruct((points, embed), F32)),
        in_specs=[pl.BlockSpec(memory_space=pl.ANY)] * 5,
        out_specs=[pl.BlockSpec(memory_space=pltpu.VMEM)] * 2,
        scratch_shapes=[
            vmem((points,), jnp.int32), vmem((probes, points), BF16), vmem((probes, points), BF16),
            vmem((chips, width), BF16), vmem((width, embed), BF16), vmem((chips, embed), BF16),
            vmem((width // 2, points), BF16), vmem((2, 2) + block, BF16), vmem((2,) + block, BF16),
            vmem((2,) + block, BF16), vmem((2, PLANE) + block, BF16), vmem((2, PLANE) + block, BF16),
            vmem((2, PLANE, 8, half), F32), vmem((NZ,) + block, BF16), vmem((NZ,) + block, BF16),
            vmem((NZ,) + block, F32), vmem((NZ,) + block, F32), vmem((NZ,) + block, F32),
            vmem((NZ,) + block, BF16), vmem((NZ,) + block, BF16), vmem((2,) + block, F32),
            vmem((PLANE, rows, embed), BF16), vmem((PLANE, rows, embed), BF16),
            vmem((NZ, rows, embed), BF16), vmem((2, PLANE, rows, embed), BF16),
            dma((4,)), dma((4,)), dma((2,)),
            dma((PLANE,)), dma((PLANE,)), dma((PLANE,)), dma((PLANE,)),
            dma((PLANE,)), dma((PLANE,)), dma((PLANE,)), dma((PLANE,)),
            dma((NZ,)), dma((NZ,)), dma((NZ,)), dma((NZ,)), dma((NZ,)), dma((NZ,)), dma((2,)),
            dma((PLANE,)), dma((PLANE,)), dma((NZ,)), dma((NZ,)),
            dma((PLANE,)), dma((PLANE,)), dma((PLANE,)), dma((PLANE,)),
        ],
        compiler_params=pltpu.CompilerParams(
            collective_id=0, has_side_effects=True, vmem_limit_bytes=60 * 2**20),
    )(batch_index, chip_features, head_weight, probe_left.T, probe_right.T)
    return pl.pallas_call(
        finish,
        out_shape=(jax.ShapeDtypeStruct((points, embed), F32), jax.ShapeDtypeStruct((width, embed), F32)),
        in_specs=[pl.BlockSpec(memory_space=pl.ANY)] * 2,
        out_specs=[pl.BlockSpec(memory_space=pl.ANY)] * 2,
        scratch_shapes=[
            vmem((width, embed), BF16), vmem((width, embed), F32), vmem((points, embed), F32), dma((5,)), dma((5,))],
    )(head, grad)


def solution(mesh):
    return jax.shard_map(
        local,
        mesh=mesh,
        in_specs=(P(("row", "col")), P(("row", "col"), None), P(), P(("row", "col"), "cores"), P(("row", "col"), "cores")),
        out_specs=(P(("row", "col"), None), P()),
        check_vma=False,
    )
```

time: 84 us -> 67.3 us (0.80)
  Pallas kernels: 76.7 us -> 66.3 us
  local copies, waits for them, and re-layouts: 6.41 us -> 0 us
    pallas_call x1, Pallas kernels: 74.6 us -> 64.3 us  [local(): pl.pallas_call(functools.partial(fused, norm), out_shape=(jax.ShapeDtypeS...]
    unnamed x12 -> x0, local copies, waits for them, and re-layouts: 6.41 us -> none
where the time goes in v2:
time: 67.3 us; the launch traced here: 67.1 us
  Pallas kernels  66.3 us (99%)
  between operations  0.8 us (1%)
    pallas_call x1, Pallas kernels, local(): pl.pallas_call(functools.partial(fused, norm), out_shape=(jax.ShapeDtypeS...  64.3 us
    pallas_call x1, Pallas kernels, local(): pl.pallas_call(finish, out_shape=(jax.ShapeDtypeStruct((points, embed), F...  2.01 us

profile of v2, /device:TPU:1, one launch (start us, length us, event | category | flops | bytes accessed | tf_op | source)
XLA Modules:
  0.0 67.1 jit_solution(16082662232301927762)
XLA Ops:
  0.6 64.3 %shard_map.68 = (bf16[2048,128]{1,0:T(8,128)(2,1)}, f32[256,128]{1,0:T(8,128)}) custom-call(s32[256]{0:T(256)} %idx_hbm.1, bf16[512,2048]{1,0:T(8,128)(2,1)} %feat_hbm.1, bf16[2048,128]{1,0:T(8,128)(2,1)} %w_hbm.1, bf16[32,256]{1,0:T(8,128)(2,1)} %bitcast.2, bf16[32,256]{1,0:T(8,128)(2,1)} %bitcast.3), custom_call_target="tpu_custom_call" | custom-call | tf_op jit(solution)/shard_map/pallas_call | solution.py:355
  64.9 2.0 %shard_map.69 = (f32[256,128]{1,0:T(8,128)}, f32[2048,128]{1,0:T(8,128)}) custom-call(bf16[2048,128]{1,0:T(8,128)(2,1)} %get-tuple-element.4.head_in, f32[256,128]{1,0:T(8,128)} %get-tuple-element.5.embed_in), custom_call_target="tpu_custom_call" | custom-call | tf_op jit(solution)/shard_map/pallas_call | solution.py:380

commit v3 on v2

v3 whole, which is shorter than its diff:
```python
import functools
import math

import jax
import jax.numpy as jnp
from jax import lax
from jax.experimental import pallas as pl
from jax.experimental.pallas import tpu as pltpu
from jax.sharding import PartitionSpec as P

MESH = pl.DeviceIdType.MESH
F32, BF16 = jnp.float32, jnp.bfloat16
NX, NY, NZ = 4, 4, 8
PLANE = NX * NY


def dot(a, b, ca, cb):
    return lax.dot_general(a, b, (((ca,), (cb,)), ((), ())), preferred_element_type=F32)


def squares(z):
    zf = z.astype(F32)
    sq = zf * zf
    hi = sq.astype(BF16)
    return hi, (sq - hi.astype(F32)).astype(BF16)


def fused(norm, idx_hbm, feat_hbm, w_hbm, left_hbm, right_hbm, head_out, embed_out,
          idx_ref, left_ref, right_ref, feat, w, e_all, ft, u_buf, u_in, z_own, zA, lrA, qA, zB, rlB, qB, acc, mass,
          gs, gr, gfull, hp, hr, hz, hb,
          feat_sem, in_sem, u_sem, az_s, az_r, al_s, al_r, fz_s, fz_r, fl_s, fl_r,
          bz_s, bz_r, bl_s, bl_r, g_s, g_r, gx_sem, hr_s, hr_r, hz_s, hz_r, ha_s, ha_r, hf_s, hf_r):
    row, col, core = lax.axis_index("row"), lax.axis_index("col"), lax.axis_index("cores")
    x, y, z = (row // NZ) * 2 + col // NY, col % NY, row % NZ
    half = z_own.shape[1]
    embed = z_own.shape[2]
    scale = 0.5 / embed * math.log2(math.e)

    def at(dx, dy, dz, dc):
        nx, ny, nz = (x + dx) % NX, (y + dy) % NY, (z + dz) % NZ
        return ((nx // 2) * NZ + nz, (nx % 2) * NY + ny, (core + dc) % 2)

    def plane_at(n):
        return at(n // NY, n % NY, 0, 0)

    def remote(src, dst, ssem, rsem, device):
        return pltpu.make_async_remote_copy(
            src_ref=src, dst_ref=dst, send_sem=ssem, recv_sem=rsem, device_id=device, device_id_type=MESH)

    sibling = at(0, 0, 0, 1)
    me_plane = x * NY + y
    other = 1 - core

    near = (1, 3, 2)
    axes = [0] + [NY * d for d in near] + list(near)
    diagonal = [NY * d + e for d in near for e in near]
    order = axes + [PLANE + n for n in axes] + diagonal + [PLANE + n for n in diagonal]
    own = [order.index(n) for n in range(PLANE)]
    passed = [order.index(PLANE + n) for n in range(PLANE)]
    line = [(j + NZ // 2) % NZ for j in range(NZ)]
    early = 2 * len(axes)

    chunk = feat.shape[0] // 4
    small_copies = [
        pltpu.make_async_copy(src, dst, in_sem.at[i])
        for i, (src, dst) in enumerate(((left_hbm, left_ref), (right_hbm, right_ref), (idx_hbm, idx_ref), (w_hbm, w)))]
    for c in small_copies:
        c.start()
    feat_copies = [
        pltpu.make_async_copy(feat_hbm.at[pl.ds(i * chunk, chunk)], feat.at[pl.ds(i * chunk, chunk)], feat_sem.at[i])
        for i in range(4)]
    for c in feat_copies:
        c.start()

    barrier = pltpu.get_barrier_semaphore()
    for n in range(1, PLANE):
        pl.semaphore_signal(barrier, inc=1, device_id=plane_at(n), device_id_type=MESH)
    for j in range(1, NZ):
        pl.semaphore_signal(barrier, inc=1, device_id=at(0, 0, j, 0), device_id_type=MESH)
    pl.semaphore_signal(barrier, inc=1, device_id=sibling, device_id_type=MESH)

    probes = left_ref.shape[0]
    lane = lax.broadcasted_iota(jnp.int32, (probes, embed), 1)
    sub = lax.broadcasted_iota(jnp.int32, (probes, embed), 0)
    first = (lane == sub + 2 * probes * core).astype(F32).astype(BF16)
    second = (lane == sub + 2 * probes * core + probes).astype(F32).astype(BF16)
    small_copies[0].wait()
    small_copies[1].wait()
    lv, rv = left_ref[...], right_ref[...]
    u = (dot(lv, first, 0, 0) + dot(rv, second, 0, 0)).astype(BF16)
    v = (dot(lv, second, 0, 0) + dot(rv, first, 0, 0)).astype(BF16)
    for h in range(2):
        u_buf[h, 0] = u[h * half:(h + 1) * half]
        u_buf[h, 1] = v[h * half:(h + 1) * half]

    small_copies[3].wait()
    for i, c in enumerate(feat_copies):
        c.wait()
        e_all[pl.ds(i * chunk, chunk)] = dot(feat[pl.ds(i * chunk, chunk)], w[...], 1, 0).astype(BF16)

    pl.semaphore_wait(barrier, PLANE - 1 + NZ - 1 + 1)

    sends = []

    def send(src, dst, ssem, rsem, device):
        c = remote(src, dst, ssem, rsem, device)
        c.start()
        sends.append(c)
        return c

    u_copy = send(u_buf.at[other], u_in, u_sem.at[0], u_sem.at[1], sibling)

    small_copies[2].wait()
    index = idx_ref[...].reshape(1, 2 * half)
    onehot = (lax.broadcasted_iota(jnp.int32, (feat.shape[0], 2 * half), 0) == index).astype(F32).astype(BF16)
    z_all = dot(onehot, e_all[...], 0, 0).astype(BF16)
    z_own[0] = z_all[:half]
    z_own[1] = z_all[half:]
    mine = z_own[core]
    zA[own[0]] = mine
    zA[passed[0]] = z_own[other]
    zB[line[0]] = mine

    def send_z(n, m):
        return send(zA.at[own[n]], zA.at[own[m]], az_s.at[m], az_r.at[m], plane_at(m - n))

    def send_l(n, m):
        return send(lrA.at[own[n]], lrA.at[own[m]], al_s.at[m], al_r.at[m], plane_at(m - n))

    def line_z(i, j):
        return send(zB.at[line[i]], zB.at[line[j]], bz_s.at[j], bz_r.at[j], at(0, 0, (j - i) % NZ, 0))

    def line_l(i, j):
        return send(rlB.at[line[i]], rlB.at[line[j]], bl_s.at[j], bl_r.at[j], at(0, 0, (j - i) % NZ, 0))

    def arrived(buf, sem):
        remote(buf, buf, sem, sem, sibling).wait_recv()

    for d in near:
        send_z(0, NY * d)
    line_z(0, 2)
    line_z(0, 6)
    for d in near:
        send_z(0, d)
    line_z(0, 1)
    line_z(0, 7)
    u_copy.wait_recv()
    lrA[own[0]] = u_buf[core, 0] + u_in[0]
    rlB[line[0]] = u_buf[core, 1] + u_in[1]
    for d in near:
        send_l(0, d)
    line_l(0, 2)
    line_l(0, 6)
    for d in near:
        send_l(0, NY * d)
    line_l(0, 1)
    line_l(0, 7)

    def forward_z(n):
        return remote(zA.at[own[n]], zA.at[passed[n]], fz_s.at[n], fz_r.at[n], sibling)

    def forward_l(n):
        return remote(lrA.at[own[n]], lrA.at[passed[n]], fl_s.at[n], fl_r.at[n], sibling)

    forward_l(0).start()
    ones = jnp.ones((8, embed), BF16)
    wide = jnp.ones((embed, embed), BF16)

    def norms_a(p, count):
        hi, lo = squares(zA[p:p + count].reshape(count * half, embed))
        q = (dot(ones, hi, 1, 1) + dot(ones, lo, 1, 1)) * scale
        for i in range(count):
            qA[p + i] = q[:, i * half:(i + 1) * half]

    def norms_b(p, count):
        hi, lo = squares(zB[p:p + count].reshape(count * half, embed))
        qB[p:p + count] = ((dot(hi, wide, 1, 0) + dot(lo, wide, 1, 0)) * scale).reshape(count, half, embed)

    for d in near:
        arrived(zA.at[own[NY * d]], az_r.at[NY * d])
        for e in near:
            send_z(NY * d, NY * d + e)
        forward_z(NY * d).start()
    arrived(zB.at[line[2]], bz_r.at[2])
    line_z(2, 3)
    line_z(2, 4)
    arrived(zB.at[line[6]], bz_r.at[6])
    line_z(6, 5)
    for d in near:
        arrived(lrA.at[own[d]], al_r.at[d])
        for e in near:
            send_l(d, NY * e + d)
        forward_l(d).start()
    arrived(rlB.at[line[2]], bl_r.at[2])
    line_l(2, 3)
    arrived(rlB.at[line[6]], bl_r.at[6])
    line_l(6, 5)
    line_l(6, 4)
    for d in near:
        arrived(zA.at[own[d]], az_r.at[d])
        forward_z(d).start()
        arrived(lrA.at[own[NY * d]], al_r.at[NY * d])
        forward_l(NY * d).start()
    for j in (1, 7):
        arrived(zB.at[line[j]], bz_r.at[j])
        arrived(rlB.at[line[j]], bl_r.at[j])

    def tile(p, count, s, blocks, first):
        rows = blocks * half
        zb = zB[s:s + blocks].reshape(rows, embed)
        rl = rlB[s:s + blocks].reshape(rows, embed)
        qb = qB[s:s + blocks].reshape(rows, embed)
        za = zA[p:p + count].reshape(count * half, embed)
        lr = lrA[p:p + count].reshape(count * half, embed)
        qa = jnp.concatenate([qA[p + i, 0:1] for i in range(count)], axis=1)
        products = dot(zb, za, 1, 1)
        pairs = dot(rl, lr, 1, 1)
        weight = jnp.exp2(products * (2.0 * scale) - (jnp.concatenate([qb] * count, axis=1) + qa)) * pairs
        part = dot(weight.astype(BF16), za, 1, 0).reshape(blocks, half, embed)
        row_mass = weight[:, :half]
        for i in range(1, count):
            row_mass = row_mass + weight[:, i * half:(i + 1) * half]
        row_mass = row_mass.reshape(blocks, half, embed)
        if first:
            acc[s:s + blocks] = part
            mass[s:s + blocks] = row_mass
        else:
            acc[s:s + blocks] += part
            mass[s:s + blocks] += row_mass

    norms_b(line[6], 4)
    norms_a(0, len(axes))
    for n in axes:
        if n:
            arrived(zA.at[passed[n]], fz_r.at[n])
        arrived(lrA.at[passed[n]], fl_r.at[n])
    norms_a(len(axes), len(axes))
    tile(0, early, line[6], 4, True)

    for n in diagonal:
        arrived(zA.at[own[n]], az_r.at[n])
        forward_z(n).start()
        arrived(lrA.at[own[n]], al_r.at[n])
        forward_l(n).start()
    norms_a(early, len(diagonal))
    for j in (3, 5, 4):
        arrived(zB.at[line[j]], bz_r.at[j])
        arrived(rlB.at[line[j]], bl_r.at[j])
    norms_b(line[4], 2)
    norms_b(line[2], 2)
    tile(0, early, line[4], 2, True)
    for n in diagonal:
        arrived(zA.at[passed[n]], fz_r.at[n])
        arrived(lrA.at[passed[n]], fl_r.at[n])
    norms_a(early + len(diagonal), len(diagonal))

    g_copies = [None] + [remote(gs.at[j], gr.at[j], g_s.at[j], g_r.at[j], at(0, 0, NZ - j, 0)) for j in range(1, NZ)]
    for j in (4, 2, 6, 0):
        s = line[j]
        if j == 2:
            tile(0, early, s, 2, True)
        tile(early, 2 * len(diagonal), s, 2, False)
        for i in (1, 0):
            total = jnp.sum(mass[s + i], axis=1, keepdims=True)
            grad = (acc[s + i] - total * zB[s + i].astype(F32)) * (1.0 / embed)
            if j + i == 0:
                acc[s] = grad
            else:
                gs[j + i] = grad.astype(BF16)
                g_copies[j + i].start()

    columns = feat.shape[1] // 2
    mine_t = feat[:, pl.ds(pl.multiple_of(core * columns, columns), columns)]
    ft[...] = dot(mine_t, onehot, 0, 0).astype(BF16)

    for c in sends:
        c.wait_send()
    for n in range(PLANE):
        if n:
            forward_z(n).wait_send()
        forward_l(n).wait_send()

    grad = acc[line[0]]
    for j in range(1, NZ):
        g_copies[j].wait_recv()
        grad = grad + gr[j].astype(F32)
    gfull[core] = grad
    gx = remote(gfull.at[core], gfull.at[core], gx_sem.at[0], gx_sem.at[1], sibling)
    gx.start()

    def head_product(which, value):
        hi = value.astype(BF16)
        lo = (value - hi.astype(F32)).astype(BF16)
        lanes = pl.ds(pl.multiple_of(which * half, half), half)
        return dot(ft[:, lanes], jnp.concatenate([hi, lo], axis=1), 1, 0)

    mine = head_product(core, grad)
    for j in range(1, NZ):
        g_copies[j].wait_send()
    gx.wait()
    product = mine + head_product(other, gfull[other])
    hp[...] = (product[:, :embed] + product[:, embed:]).astype(BF16).reshape(hp.shape)

    def slice_of(n):
        return ((x + n // NY) % NX) * NY + (y + n % NY) % NY

    hr_copies = [None] + [remote(hp.at[slice_of(n)], hr.at[n], hr_s.at[n], hr_r.at[n], plane_at(n)) for n in range(1, PLANE)]
    by_distance = sorted(range(PLANE), key=lambda n: min(n // NY, NX - n // NY) + min(n % NY, NY - n % NY))
    for n in by_distance[:0:-1]:
        hr_copies[n].start()
    embed_out[...] = gfull[...].reshape(2 * half, embed)
    total = hp[me_plane].astype(F32)
    for n in by_distance[1:]:
        hr_copies[n].wait_recv()
        total = total + hr[n].astype(F32)
    hz[z] = (total * norm).astype(BF16)

    hz_copies = [None] + [remote(hz.at[z], hz.at[z], hz_s.at[j], hz_r.at[j], at(0, 0, j, 0)) for j in range(1, NZ)]
    for j in range(1, NZ):
        hz_copies[j].start()
    for n in range(1, PLANE):
        hr_copies[n].wait_send()
    for j in range(1, NZ):
        hz_copies[j].wait_recv()
    total = hz[0].astype(F32)
    for j in range(1, NZ):
        total = total + hz[j].astype(F32)
    hb[core, me_plane] = total.astype(BF16)

    ha_copies = [None] + [
        remote(hb.at[core, me_plane], hb.at[core, me_plane], ha_s.at[n], ha_r.at[n], plane_at(n)) for n in range(1, PLANE)]
    for n in by_distance[:0:-1]:
        ha_copies[n].start()
    hf_copies = []
    for n in by_distance:
        source = ((x + NX - n // NY) % NX) * NY + (y + NY - n % NY) % NY
        if n:
            ha_copies[n].wait_recv()
        c = remote(hb.at[core, source], hb.at[core, source], hf_s.at[n], hf_r.at[n], sibling)
        c.start()
        hf_copies.append(c)
    for j in range(1, NZ):
        hz_copies[j].wait_send()
    for n in range(1, PLANE):
        ha_copies[n].wait_send()
    for c in hf_copies:
        c.wait()
    head_out[...] = hb[...].reshape(head_out.shape)


def finish(head_in, embed_in, embed_out, head_out, head_f, out_sem):
    pieces = out_sem.shape[0] - 1
    rows = head_f.shape[0] // pieces
    embed_store = pltpu.make_async_copy(embed_in, embed_out, out_sem.at[pieces])
    embed_store.start()
    stores = []
    for i in range(pieces):
        cut = pl.ds(i * rows, rows)
        head_f[cut] = head_in[cut].astype(F32)
        stores.append(pltpu.make_async_copy(head_f.at[cut], head_out.at[cut], out_sem.at[i]))
        stores[i].start()
    for c in stores:
        c.wait()
    embed_store.wait()


def local(batch_index, chip_features, head_weight, probe_left, probe_right):
    points = batch_index.shape[0]
    half = points // 2
    chips, width = chip_features.shape
    probes = probe_left.shape[1]
    embed = head_weight.shape[1]
    rows = width // 2 // PLANE
    norm = 1.0 / math.sqrt(points * PLANE * NZ)
    block = (half, embed)
    vmem, dma = pltpu.VMEM, pltpu.SemaphoreType.DMA
    head, grad = pl.pallas_call(
        functools.partial(fused, norm),
        out_shape=(jax.ShapeDtypeStruct((width, embed), BF16), jax.ShapeDtypeStruct((points, embed), F32)),
        in_specs=[pl.BlockSpec(memory_space=pl.ANY)] * 5,
        out_specs=[pl.BlockSpec(memory_space=pltpu.VMEM)] * 2,
        scratch_shapes=[
            vmem((points,), jnp.int32), vmem((probes, points), BF16), vmem((probes, points), BF16),
            vmem((chips, width), BF16), vmem((width, embed), BF16), vmem((chips, embed), BF16),
            vmem((width // 2, points), BF16), vmem((2, 2) + block, BF16), vmem((2,) + block, BF16),
            vmem((2,) + block, BF16), vmem((2 * PLANE,) + block, BF16), vmem((2 * PLANE,) + block, BF16),
            vmem((2 * PLANE, 8, half), F32), vmem((NZ,) + block, BF16), vmem((NZ,) + block, BF16),
            vmem((NZ,) + block, F32), vmem((NZ,) + block, F32), vmem((NZ,) + block, F32),
            vmem((NZ,) + block, BF16), vmem((NZ,) + block, BF16), vmem((2,) + block, F32),
            vmem((PLANE, rows, embed), BF16), vmem((PLANE, rows, embed), BF16),
            vmem((NZ, rows, embed), BF16), vmem((2, PLANE, rows, embed), BF16),
            dma((4,)), dma((4,)), dma((2,)),
            dma((PLANE,)), dma((PLANE,)), dma((PLANE,)), dma((PLANE,)),
            dma((PLANE,)), dma((PLANE,)), dma((PLANE,)), dma((PLANE,)),
            dma((NZ,)), dma((NZ,)), dma((NZ,)), dma((NZ,)), dma((NZ,)), dma((NZ,)), dma((2,)),
            dma((PLANE,)), dma((PLANE,)), dma((NZ,)), dma((NZ,)),
            dma((PLANE,)), dma((PLANE,)), dma((PLANE,)), dma((PLANE,)),
        ],
        compiler_params=pltpu.CompilerParams(
            collective_id=0, has_side_effects=True, vmem_limit_bytes=48 * 2**20),
    )(*(pltpu.with_memory_space_constraint(a, pltpu.HBM)
        for a in (batch_index, chip_features, head_weight, probe_left.T, probe_right.T)))
    return pl.pallas_call(
        finish,
        out_shape=(jax.ShapeDtypeStruct((points, embed), F32), jax.ShapeDtypeStruct((width, embed), F32)),
        in_specs=[pl.BlockSpec(memory_space=pltpu.VMEM)] * 2,
        out_specs=[pl.BlockSpec(memory_space=pl.ANY)] * 2,
        scratch_shapes=[vmem((width, embed), F32), dma((5,))],
        compiler_params=pltpu.CompilerParams(vmem_limit_bytes=4 * 2**20),
    )(head, grad)


def solution(mesh):
    return jax.shard_map(
        local,
        mesh=mesh,
        in_specs=(P(("row", "col")), P(("row", "col"), None), P(), P(("row", "col"), "cores"), P(("row", "col"), "cores")),
        out_specs=(P(("row", "col"), None), P()),
        check_vma=False,
    )
```

time: 67.3 us -> 58.5 us (0.87)
  Pallas kernels: 66.3 us -> 57.6 us
    pallas_call x1, Pallas kernels: 64.3 us -> 56.6 us  [local(): pl.pallas_call(functools.partial(fused, norm), out_shape=(jax.ShapeDtypeS...]
    pallas_call x1, Pallas kernels: 2.01 us -> 1.05 us  [local(): pl.pallas_call(finish, out_shape=(jax.ShapeDtypeStruct((points, embed), F...]
where the time goes in v3:
time: 58.5 us; the launch traced here: 58.3 us
  Pallas kernels  57.6 us (98%)
  between operations  0.64 us (1%)
    pallas_call x1, Pallas kernels, local(): pl.pallas_call(functools.partial(fused, norm), out_shape=(jax.ShapeDtypeS...  56.6 us

profile of v3, /device:TPU:1, one launch (start us, length us, event | category | flops | bytes accessed | tf_op | source)
XLA Modules:
  0.0 58.3 jit_solution(10236225520631510932)
XLA Ops:
  0.6 56.6 %shard_map.68 = (bf16[2048,128]{1,0:T(8,128)(2,1)S(1)}, f32[256,128]{1,0:T(8,128)S(1)}) custom-call(s32[256]{0:T(256)} %idx_hbm.1, bf16[512,2048]{1,0:T(8,128)(2,1)} %feat_hbm.1, bf16[2048,128]{1,0:T(8,128)(2,1)} %w_hbm.1, bf16[32,256]{1,0:T(8,128)(2,1)} %bitcast.2, bf16[32,256]{1,0:T(8,128)(2,1)} %bitcast.3), custom_call_target="tpu_custom_call" | custom-call | tf_op jit(solution)/shard_map/pallas_call | solution.py:377
  57.2 1.1 %shard_map.69 = (f32[256,128]{1,0:T(8,128)}, f32[2048,128]{1,0:T(8,128)}) custom-call(bf16[2048,128]{1,0:T(8,128)(2,1)S(1)} %get-tuple-element.4.head_in, f32[256,128]{1,0:T(8,128)S(1)} %get-tuple-element.5.embed_in), custom_call_target="tpu_custom_call" | custom-call | tf_op jit(solution)/shard_map/pallas_call | solution.py:403

commit v4 on v3

--- a/solution.py
+++ b/solution.py
@@ -237,6 +237,11 @@
     norms_a(len(axes), len(axes))
     tile(0, early, line[6], 4, True)
 
+    columns = feat.shape[1] // 2
+    mine_t = feat[:, pl.ds(pl.multiple_of(core * columns, columns), columns)]
+    ft[...] = dot(mine_t, onehot, 0, 0).astype(BF16)
+
+
     for n in diagonal:
         arrived(zA.at[own[n]], az_r.at[n])
         forward_z(n).start()
@@ -269,9 +274,35 @@
                 gs[j + i] = grad.astype(BF16)
                 g_copies[j + i].start()
 
-    columns = feat.shape[1] // 2
-    mine_t = feat[:, pl.ds(pl.multiple_of(core * columns, columns), columns)]
-    ft[...] = dot(mine_t, onehot, 0, 0).astype(BF16)
+    grad = acc[line[0]]
+    for j in range(1, NZ):
+        g_copies[j].wait_recv()
+        grad = grad + gr[j].astype(F32)
+    gfull[core] = grad
+    gx = remote(gfull.at[core], gfull.at[core], gx_sem.at[0], gx_sem.at[1], sibling)
+    gx.start()
+
+    def head_product(which, value):
+        hi = value.astype(BF16)
+        lo = (value - hi.astype(F32)).astype(BF16)
+        lanes = pl.ds(pl.multiple_of(which * half, half), half)
+        return dot(ft[:, lanes], jnp.concatenate([hi, lo], axis=1), 1, 0)
+
+    mine = head_product(core, grad)
+    for j in range(1, NZ):
+        g_copies[j].wait_send()
+    gx.wait()
+    product = mine + head_product(other, gfull[other])
+    hp[...] = (product[:, :embed] + product[:, embed:]).astype(BF16).reshape(hp.shape)
+
+    def slice_of(n):
+        return ((x + n // NY) % NX) * NY + (y + n % NY) % NY
+
+    hr_copies = [None] + [remote(hp.at[slice_of(n)], hr.at[n], hr_s.at[n], hr_r.at[n], plane_at(n)) for n in range(1, PLANE)]
+    by_distance = sorted(range(PLANE), key=lambda n: min(n // NY, NX - n // NY) + min(n % NY, NY - n % NY))
+    for n in by_distance[:0:-1]:
+        hr_copies[n].start()
+    embed_out[...] = gfull[...].reshape(2 * half, embed)
 
     for c in sends:
         c.wait_send()
@@ -280,35 +311,6 @@
             forward_z(n).wait_send()
         forward_l(n).wait_send()
 
-    grad = acc[line[0]]
-    for j in range(1, NZ):
-        g_copies[j].wait_recv()
-        grad = grad + gr[j].astype(F32)
-    gfull[core] = grad
-    gx = remote(gfull.at[core], gfull.at[core], gx_sem.at[0], gx_sem.at[1], sibling)
-    gx.start()
-
-    def head_product(which, value):
-        hi = value.astype(BF16)
-        lo = (value - hi.astype(F32)).astype(BF16)
-        lanes = pl.ds(pl.multiple_of(which * half, half), half)
-        return dot(ft[:, lanes], jnp.concatenate([hi, lo], axis=1), 1, 0)
-
-    mine = head_product(core, grad)
-    for j in range(1, NZ):
-        g_copies[j].wait_send()
-    gx.wait()
-    product = mine + head_product(other, gfull[other])
-    hp[...] = (product[:, :embed] + product[:, embed:]).astype(BF16).reshape(hp.shape)
-
-    def slice_of(n):
-        return ((x + n // NY) % NX) * NY + (y + n % NY) % NY
-
-    hr_copies = [None] + [remote(hp.at[slice_of(n)], hr.at[n], hr_s.at[n], hr_r.at[n], plane_at(n)) for n in range(1, PLANE)]
-    by_distance = sorted(range(PLANE), key=lambda n: min(n // NY, NX - n // NY) + min(n % NY, NY - n % NY))
-    for n in by_distance[:0:-1]:
-        hr_copies[n].start()
-    embed_out[...] = gfull[...].reshape(2 * half, embed)
     total = hp[me_plane].astype(F32)
     for n in by_distance[1:]:
         hr_copies[n].wait_recv()
@@ -316,7 +318,7 @@
     hz[z] = (total * norm).astype(BF16)
 
     hz_copies = [None] + [remote(hz.at[z], hz.at[z], hz_s.at[j], hz_r.at[j], at(0, 0, j, 0)) for j in range(1, NZ)]
-    for j in range(1, NZ):
+    for j in (4, 3, 5, 2, 6, 1, 7):
         hz_copies[j].start()
     for n in range(1, PLANE):
         hr_copies[n].wait_send()

time: 58.5 us -> 57.8 us (0.988)
  Pallas kernels: 57.6 us -> 57 us
    pallas_call x1, Pallas kernels: 56.6 us -> 56 us  [local(): pl.pallas_call(functools.partial(fused, norm), out_shape=(jax.ShapeDtypeS...]
where the time goes in v4:
time: 57.8 us; the launch traced here: 57.7 us
  Pallas kernels  57 us (99%)
  between operations  0.64 us (1%)
    pallas_call x1, Pallas kernels, local(): pl.pallas_call(functools.partial(fused, norm), out_shape=(jax.ShapeDtypeS...  56 us

profile of v4, /device:TPU:1, one launch (start us, length us, event | category | flops | bytes accessed | tf_op | source)
XLA Modules:
  0.0 57.7 jit_solution(5339650838308288148)
XLA Ops:
  0.6 56.0 %shard_map.68 = (bf16[2048,128]{1,0:T(8,128)(2,1)S(1)}, f32[256,128]{1,0:T(8,128)S(1)}) custom-call(s32[256]{0:T(256)} %idx_hbm.1, bf16[512,2048]{1,0:T(8,128)(2,1)} %feat_hbm.1, bf16[2048,128]{1,0:T(8,128)(2,1)} %w_hbm.1, bf16[32,256]{1,0:T(8,128)(2,1)} %bitcast.2, bf16[32,256]{1,0:T(8,128)(2,1)} %bitcast.3), custom_call_target="tpu_custom_call" | custom-call | tf_op jit(solution)/shard_map/pallas_call | solution.py:379
  56.6 1.1 %shard_map.69 = (f32[256,128]{1,0:T(8,128)}, f32[2048,128]{1,0:T(8,128)}) custom-call(bf16[2048,128]{1,0:T(8,128)(2,1)S(1)} %get-tuple-element.4.head_in, f32[256,128]{1,0:T(8,128)S(1)} %get-tuple-element.5.embed_in), custom_call_target="tpu_custom_call" | custom-call | tf_op jit(solution)/shard_map/pallas_call | solution.py:405

commit v5 on v4

--- a/solution.py
+++ b/solution.py
@@ -228,14 +228,14 @@
             acc[s:s + blocks] += part
             mass[s:s + blocks] += row_mass
 
-    norms_b(line[6], 4)
+    norms_b(line[6], 5)
     norms_a(0, len(axes))
     for n in axes:
         if n:
             arrived(zA.at[passed[n]], fz_r.at[n])
         arrived(lrA.at[passed[n]], fl_r.at[n])
     norms_a(len(axes), len(axes))
-    tile(0, early, line[6], 4, True)
+    tile(0, early, line[6], 5, True)
 
     columns = feat.shape[1] // 2
     mine_t = feat[:, pl.ds(pl.multiple_of(core * columns, columns), columns)]
@@ -252,7 +252,7 @@
         arrived(zB.at[line[j]], bz_r.at[j])
         arrived(rlB.at[line[j]], bl_r.at[j])
     norms_b(line[4], 2)
-    norms_b(line[2], 2)
+    norms_b(line[3], 1)
     tile(0, early, line[4], 2, True)
     for n in diagonal:
         arrived(zA.at[passed[n]], fz_r.at[n])
@@ -263,7 +263,7 @@
     for j in (4, 2, 6, 0):
         s = line[j]
         if j == 2:
-            tile(0, early, s, 2, True)
+            tile(0, early, line[3], 1, True)
         tile(early, 2 * len(diagonal), s, 2, False)
         for i in (1, 0):
             total = jnp.sum(mass[s + i], axis=1, keepdims=True)

time: 57.8 us -> 58 us (level)
  no operation moved by 1% of the time
where the time goes in v5:
time: 58 us; the launch traced here: 57.8 us
  Pallas kernels  57.2 us (99%)
  between operations  0.64 us (1%)
    pallas_call x1, Pallas kernels, local(): pl.pallas_call(functools.partial(fused, norm), out_shape=(jax.ShapeDtypeS...  56.1 us

profile of v5, /device:TPU:1, one launch (start us, length us, event | category | flops | bytes accessed | tf_op | source)
XLA Modules:
  0.0 57.8 jit_solution(2710883166494755801)
XLA Ops:
  0.6 56.1 %shard_map.68 = (bf16[2048,128]{1,0:T(8,128)(2,1)S(1)}, f32[256,128]{1,0:T(8,128)S(1)}) custom-call(s32[256]{0:T(256)} %idx_hbm.1, bf16[512,2048]{1,0:T(8,128)(2,1)} %feat_hbm.1, bf16[2048,128]{1,0:T(8,128)(2,1)} %w_hbm.1, bf16[32,256]{1,0:T(8,128)(2,1)} %bitcast.2, bf16[32,256]{1,0:T(8,128)(2,1)} %bitcast.3), custom_call_target="tpu_custom_call" | custom-call | tf_op jit(solution)/shard_map/pallas_call | solution.py:379
  56.8 1.1 %shard_map.69 = (f32[256,128]{1,0:T(8,128)}, f32[2048,128]{1,0:T(8,128)}) custom-call(bf16[2048,128]{1,0:T(8,128)(2,1)S(1)} %get-tuple-element.4.head_in, f32[256,128]{1,0:T(8,128)S(1)} %get-tuple-element.5.embed_in), custom_call_target="tpu_custom_call" | custom-call | tf_op jit(solution)/shard_map/pallas_call | solution.py:405
